TPU v7x, 128 devices: a whole 4x4x4 slice. The times are simulated.
128 devices in a mesh: row: 4 (over x_hi, core), col: 32 (over y, x_lo, z).
Axes of the slice: x: 4 (x_hi: 2, x_lo: 2; x = x_hi * 2 + x_lo), y: 4, z: 4, core: 2. Of those that a mesh axis runs over, the one named last changes fastest.
Arguments:
- adjusted_weight: bfloat16 [8192, 53248], P('row', 'col'), may hold values from -0.05416994 to 0.05416994
- base_weight: bfloat16 [8192, 53248], P('row', 'col'), may hold values from -0.026434931 to 0.026434931
- test_matrix: float32 [53248, 512], P('col'), may hold values from -6 to 6
Outputs:
- basis: float32 [8192, 512], P(('row', 'col'))
All inputs are finite; a program needn't handle non-finite values.
Results may differ from a plain program's by a relative error of at most 0.0015.
Values sent between devices are 32-bit elements; how exact they have to be, the bound alone decides.
A program may use at most 128 MiB of HBM per device.

v0:
```python
import jax
import jax.numpy as jnp
from jax import lax
from jax.sharding import PartitionSpec as P

M = 8192


def gram_factor(sketch_rows):
    gram_matrix = jnp.einsum("ik,il->kl", sketch_rows, sketch_rows, precision=lax.Precision.HIGHEST)
    summed = lax.psum(gram_matrix, ("row", "col"))
    return jnp.linalg.cholesky(summed)


def apply_inverse(factor_low, sketch_rows):
    return lax.linalg.triangular_solve(
        factor_low, sketch_rows, left_side=False, lower=True, transpose_a=True
    )


def column_sum(partial_sketch):
    return lax.psum(partial_sketch, "col")


def shards(adjusted_weight, base_weight, test_matrix):
    delta_full = adjusted_weight.astype(jnp.float32) - base_weight.astype(jnp.float32)
    local_rows = delta_full.shape[0]
    local_cols = delta_full.shape[1]
    share_rows = local_rows // lax.axis_size("col")
    share_cols = local_cols // lax.axis_size("row")
    scale_out = jnp.sqrt(jnp.float32(M))
    sketch = column_sum(
        jnp.dot(
            delta_full,
            test_matrix,
            precision=lax.Precision.HIGHEST,
            preferred_element_type=jnp.float32,
        )
    )
    own_offset = lax.axis_index("col") * share_rows
    factor_low = gram_factor(lax.dynamic_slice_in_dim(sketch, own_offset, share_rows, 0))
    first_basis = apply_inverse(factor_low, sketch)
    cosketch = lax.psum(
        jnp.einsum("mn,mk->nk", delta_full, first_basis, precision=lax.Precision.HIGHEST), "row"
    )
    col_offset = lax.axis_index("row") * share_cols
    factor_low = gram_factor(lax.dynamic_slice_in_dim(cosketch, col_offset, share_cols, 0))
    second_basis = apply_inverse(factor_low, cosketch)
    resketch = column_sum(
        jnp.dot(
            delta_full,
            second_basis,
            precision=lax.Precision.HIGHEST,
            preferred_element_type=jnp.float32,
        )
    )
    own_rows = lax.dynamic_slice_in_dim(resketch, own_offset, share_rows, 0)
    factor_low = gram_factor(own_rows)
    return scale_out * apply_inverse(factor_low, own_rows)


def solution(mesh):
    return jax.shard_map(
        shards,
        mesh=mesh,
        in_specs=(P("row", "col"), P("row", "col"), P("col", None)),
        out_specs=P(("row", "col"), None),
        check_vma=False,
    )
```

profile of v0, /device:TPU:1, one launch (start us, length us, event | category | flops | bytes accessed | tf_op | source)
XLA Modules:
  0.0 1774.9 jit_solution(12276546253616300450)
XLA Ops:
  8.5 27.5 %fusion.2 = f32[2048,512]{1,0:T(8,128)} fusion(f32[1664,512]{1,0:T(8,128)S(1)} %copy-done, bf16[2048,1664]{1,0:T(8,128)(2,1)} %param.5, bf16[2048,1664]{1,0:T(8,128)(2,1)} %param.4), kind=kOutput, calls=%fused_computation.9 | convolution fusion | flops 20948189184 | bytes 21233664 | tf_op jit(solution)/shard_map/dot_general | solution.py:33
  36.1 303.1 %all-reduce.8.cloned.1.call-done = f32[2048,512]{1,0:T(8,128)} async-done(((f32[2048,512]{1,0:T(8,128)}), f32[2048,512]{1,0:T(8,128)}) %all-reduce.8.cloned.1.call-update) | async-done | bytes 4194320 | tf_op jit(solution)/shard_map/psum | solution.py:22
  342.8 169.8 %all-reduce.10.cloned.1.call-done = f32[512,512]{0,1:T(8,128)} async-done(((f32[512,512]{0,1:T(8,128)}), f32[512,512]{0,1:T(8,128)}) %all-reduce.10.cloned.1.call-update) | async-done | bytes 1048592 | tf_op jit(solution)/shard_map/psum | solution.py:11
  515.6 11.7 cholesky.374
  537.9 11.7 cholesky.393
  560.3 11.7 cholesky.414
  583.1 11.7 cholesky.431
  607.2 39.3 %custom-call.29 = f32[4,128,128]{1,2,0:T(8,128)S(1)} custom-call(f32[4,128,128]{2,1,0:T(8,128)S(1)} %get-tuple-element.13), custom_call_target="InvertDiagBlocksLowerTriangular" | custom-call | tf_op jit(solution)/shard_map/triangular_solve | solution.py:16
  666.6 46.5 %fusion.1 = f32[1664,512]{1,0:T(8,128)} fusion(bf16[2048,1664]{1,0:T(8,128)(2,1)S(1)} %bitcast.146, bf16[2048,1664]{1,0:T(8,128)(2,1)} %param.4, f32[2048,128]{0,1:T(8,128)S(1)} %fusion.96, f32[2048,128]{0,1:T(8,128)S(1)} %fusion.97, f32[2048,128]{0,1:T(8,128)S(1)} %fusion.98, f32[2048,128]{0,1:T(8,128)S(1)} %fusion.41), kind=kOutput, calls=%fused_computation.8 | convolution fusion | flops 20951334912 | bytes 21233664 | tf_op jit(solution)/shard_map/mn,mk->nk/dot_general | solution.py:44
  713.2 79.2 %all-reduce.12.cloned.1.call-done = f32[1664,512]{1,0:T(8,128)} async-done(((f32[1664,512]{1,0:T(8,128)}), f32[1664,512]{1,0:T(8,128)}) %all-reduce.12.cloned.1.call-update) | async-done | bytes 3407888 | tf_op jit(solution)/shard_map/psum | solution.py:43
  797.2 147.1 %all-reduce.14.cloned.1.call-done = f32[512,512]{0,1:T(8,128)} async-done(((f32[512,512]{0,1:T(8,128)}), f32[512,512]{0,1:T(8,128)}) %all-reduce.14.cloned.1.call-update) | async-done | bytes 1048592 | tf_op jit(solution)/shard_map/psum | solution.py:11
  947.3 11.7 cholesky.446
  969.7 11.7 cholesky.465
  993.4 11.7 cholesky.486
  1016.3 11.7 cholesky.503
  1039.8 39.3 %custom-call.30 = f32[4,128,128]{1,2,0:T(8,128)S(1)} custom-call(f32[4,128,128]{2,1,0:T(8,128)S(1)} %get-tuple-element.21), custom_call_target="InvertDiagBlocksLowerTriangular" | custom-call | tf_op jit(solution)/shard_map/triangular_solve | solution.py:16
  1099.1 27.1 %fusion = f32[2048,512]{1,0:T(8,128)} fusion(bf16[2048,1664]{1,0:T(8,128)(2,1)S(1)} %bitcast.148, bf16[2048,1664]{1,0:T(8,128)(2,1)} %param.4, f32[1664,128]{0,1:T(8,128)S(1)} %fusion.90, f32[1664,128]{0,1:T(8,128)S(1)} %fusion.91, f32[1664,128]{0,1:T(8,128)S(1)} %fusion.92, f32[1664,128]{0,1:T(8,128)S(1)} %fusion.46), kind=kOutput, calls=%fused_computation.7 | convolution fusion | flops 20950745088 | bytes 21233664 | tf_op jit(solution)/shard_map/dot_general | solution.py:50
  1126.4 298.6 %all-reduce.16.cloned.1.call-done = f32[2048,512]{1,0:T(8,128)} async-done(((f32[2048,512]{1,0:T(8,128)}), f32[2048,512]{1,0:T(8,128)}) %all-reduce.16.cloned.1.call-update) | async-done | bytes 4194320 | tf_op jit(solution)/shard_map/psum | solution.py:22
  1428.0 170.2 %all-reduce.18.cloned.1.call-done = f32[512,512]{0,1:T(8,128)} async-done(((f32[512,512]{0,1:T(8,128)}), f32[512,512]{0,1:T(8,128)}) %all-reduce.18.cloned.1.call-update) | async-done | bytes 1048592 | tf_op jit(solution)/shard_map/psum | solution.py:11
  1602.3 11.7 cholesky.518
  1656.6 13.2 cholesky.558
  1686.2 12.0 cholesky.575
  1705.0 13.6 while.5
  1718.6 40.7 %custom-call.31 = f32[4,128,128]{1,2,0:T(8,128)} custom-call(f32[4,128,128]{2,1,0:T(8,128)} %get-tuple-element.29), custom_call_target="InvertDiagBlocksLowerTriangular" | custom-call | tf_op jit(solution)/shard_map/triangular_solve | solution.py:16
  (178 shorter events, 249.7 us)
Async XLA Ops:
  6.5 2.0 copy-start
  6.5 332.6 %all-reduce.8.cloned.1.call-start = ((), (), s32[]{:S(2)}) async-start(), calls=%async_computation | async-start | bytes 8388608 | tf_op jit(solution)/shard_map/psum | solution.py:22
  36.0 476.5 %all-reduce.10.cloned.1.call-start = ((), (), s32[]{:S(2)}) async-start(), calls=%async_computation.1 | async-start | bytes 2097152 | tf_op jit(solution)/shard_map/psum | solution.py:11
  342.2 450.2 %all-reduce.12.cloned.1.call-start = ((), (), s32[]{:S(2)}) async-start(), calls=%async_computation.2 | async-start | bytes 6815744 | tf_op jit(solution)/shard_map/psum | solution.py:43
  607.2 41.8 %copy-start.4 = (f32[512,512]{1,0:T(8,128)}, f32[512,512]{1,0:T(8,128)S(1)}, u32[]{:S(2)}) copy-start(f32[512,512]{1,0:T(8,128)S(1)} %get-tuple-element.255) | copy-start | bytes 3145732
  646.5 6.6 copy-start.2
  653.1 13.4 slice-start
  658.8 7.7 slice-start.1
  713.2 231.1 %all-reduce.14.cloned.1.call-start = ((), (), s32[]{:S(2)}) async-start(), calls=%async_computation.3 | async-start | bytes 2097152 | tf_op jit(solution)/shard_map/psum | solution.py:11
  796.7 628.3 %all-reduce.16.cloned.1.call-start = ((), (), s32[]{:S(2)}) async-start(), calls=%async_computation.4 | async-start | bytes 8388608 | tf_op jit(solution)/shard_map/psum | solution.py:22
  1039.8 39.3 %copy-start.3 = (f32[512,512]{1,0:T(8,128)}, f32[512,512]{1,0:T(8,128)S(1)}, u32[]{:S(2)}) copy-start(f32[512,512]{1,0:T(8,128)S(1)} %get-tuple-element.253) | copy-start | bytes 3145732
  1079.2 5.9 copy-start.7
  1084.1 15.0 slice-start.2
  1089.4 9.7 slice-start.3
  1126.2 472.1 %all-reduce.18.cloned.1.call-start = ((), (), s32[]{:S(2)}) async-start(), calls=%async_computation.5 | async-start | bytes 2097152 | tf_op jit(solution)/shard_map/psum | solution.py:11
  1601.3 1.0 copy-start.5
  1615.2 152.6 %copy-start.1 = (f32[1664,512]{1,0:T(8,128)S(1)}, f32[1664,512]{1,0:T(8,128)}, u32[]{:S(2)}) copy-start(f32[1664,512]{1,0:T(8,128)} %param.6) | copy-start | bytes 10223620
  1628.2 0.7 copy-start.6
Sparse Core Ops, SparseCore 0:
  36.1 302.9 all-reduce.7
  343.9 168.5 all-reduce.9
  713.3 79.0 all-reduce.11
  797.8 146.4 all-reduce.13
  1126.3 298.6 all-reduce.15
  1429.7 168.5 all-reduce.17
where the time goes:
time: 1780 us; the launch traced here: 1770 us
  waiting for transfers between devices  1170 us (66%)
  other arithmetic  371 us (21%)
  matrix products  172 us (10%)
  local copies, waits for them, and re-layouts  40.5 us (2%)
  between operations  22 us (1%)
    psum x2, waiting for transfers between devices, column_sum(): return lax.psum(partial_sketch, 'col')  602 us
    psum x3, waiting for transfers between devices, gram_factor(): summed = lax.psum(gram_matrix, ('row', 'col'))  487 us
    another operation x44, other arithmetic, gram_factor(): return jnp.linalg.cholesky(summed)  243 us
    another operation x7, other arithmetic, apply_inverse(): lax.linalg.triangular_solve(factor_low, sketch_rows, left_side=False, low...  123 us
    psum x1, waiting for transfers between devices, shards(): lax.psum(jnp.einsum('mn,mk->nk', delta_full, first_basis, precision=lax.P...  79.2 us
    another operation x21, matrix products, apply_inverse(): lax.linalg.triangular_solve(factor_low, sketch_rows, left_side=False, low...  47.5 us
    dot_general x1, matrix products, shards(): jnp.einsum('mn,mk->nk', delta_full, first_basis, precision=lax.Precision....  46.5 us
  transfers between devices with their start and end apart: 6, of which 6 were waited for; matrix products, arithmetic and copies ran while one was open for 0% of the time, Pallas kernels for 0%

commit v1 on v0

v1 whole, which is shorter than its diff:
```python
import jax
import jax.numpy as jnp
from jax import lax
from jax.experimental import pallas as pl
from jax.experimental.pallas import tpu as pltpu
from jax.sharding import PartitionSpec as P

MESH = pl.DeviceIdType.MESH
VM = pl.BlockSpec(memory_space=pltpu.VMEM)

def place():
    r = lax.axis_index("row"); c = lax.axis_index("col")
    y = lax.div(c, 8); x = lax.rem(lax.div(c, 4), 2); z = lax.rem(c, 4)
    def dev(yy, xx, zz):
        return (r, yy*8 + xx*4 + zz)
    return r, y, x, z, dev

def barrier(devs):
    sem = pltpu.get_barrier_semaphore()
    for d in devs:
        pl.semaphore_signal(sem, inc=1, device_id=d, device_id_type=MESH)
    pl.semaphore_wait(sem, len(devs))

def rc(src, dst, ssem, rsem, dev):
    return pltpu.make_async_remote_copy(src_ref=src, dst_ref=dst, send_sem=ssem, recv_sem=rsem, device_id=dev, device_id_type=MESH)

class RingRS:
    def __init__(self, part, me, devp, devm, relay, fin, ssem, rsem):
        self.part, self.me, self.devp, self.devm, self.relay, self.fin = part, me, devp, devm, relay, fin
        up = lax.rem(me+1, 4); dn = lax.rem(me+3, 4); far = lax.rem(me+2, 4)
        self.up, self.dn = up, dn
        self.c = [
            rc(part(far, 0), relay.at[0], ssem.at[0], rsem.at[0], devp),
            rc(part(far, 1), relay.at[1], ssem.at[1], rsem.at[1], devm),
            rc(part(up, 1), fin.at[0, 1], ssem.at[2], rsem.at[2], devp),
            rc(part(dn, 0), fin.at[1, 0], ssem.at[3], rsem.at[3], devm),
            rc(relay.at[0], fin.at[0, 0], ssem.at[4], rsem.at[4], devp),
            rc(relay.at[1], fin.at[1, 1], ssem.at[5], rsem.at[5], devm),
        ]
    def start(self):
        for i in range(4): self.c[i].start()
    def forward(self):
        self.c[0].wait_recv()
        self.relay[0] = self.relay[0] + self.part(self.up, 0)[...]
        self.c[4].start()
        self.c[1].wait_recv()
        self.relay[1] = self.relay[1] + self.part(self.dn, 1)[...]
        self.c[5].start()
    def finish(self, out):
        for i in (2, 3, 4, 5): self.c[i].wait_recv()
        for h in range(2):
            out[h] = self.part(self.me, h)[...] + self.fin[0, h] + self.fin[1, h]
    def drain(self):
        for i in range(6): self.c[i].wait_send()

def rs_col_kernel(p, o, relA, finA, relB, finB, qa, qb, relA2, finA2, relB2, finB2, ra, rb, recx, ss, rs, sx, rx):
    r, y, x, z, dev = place()
    yp, ym = dev(lax.rem(y+1,4),x,z), dev(lax.rem(y+3,4),x,z)
    zp, zm = dev(y,x,lax.rem(z+1,4)), dev(y,x,lax.rem(z+3,4))
    xd = dev(y,1-x,z)
    barrier([yp, ym, zp, zm, xd])
    A = pl.ds(0,256); Bc = pl.ds(256,256)
    a1 = RingRS(lambda k,h: p.at[k,h,:,:,A], y, yp, ym, relA, finA, ss.at[0], rs.at[0])
    b1 = RingRS(lambda k,h: p.at[:,h,k,:,Bc], z, zp, zm, relB, finB, ss.at[1], rs.at[1])
    a1.start(); b1.start(); a1.forward(); b1.forward()
    a1.finish(qa)
    a2 = RingRS(lambda k,h: qa.at[h,k], z, zp, zm, relA2, finA2, ss.at[2], rs.at[2])
    a2.start()
    b1.finish(qb)
    b2 = RingRS(lambda k,h: qb.at[h,k], y, yp, ym, relB2, finB2, ss.at[3], rs.at[3])
    b2.start()
    a2.forward(); b2.forward()
    a2.finish(ra)
    cxa = rc(ra.at[1-x], recx.at[0], sx.at[0], rx.at[0], xd); cxa.start()
    b2.finish(rb)
    cxb = rc(rb.at[1-x], recx.at[1], sx.at[1], rx.at[1], xd); cxb.start()
    cxa.wait_recv()
    o[:, 0:256] = ra[x] + recx[0]
    cxb.wait_recv()
    o[:, 256:512] = rb[x] + recx[1]
    for t in (a1, b1, a2, b2): t.drain()
    cxa.wait_send(); cxb.wait_send()

def rs_col(p, cid=1):
    S = 64
    f = jnp.float32
    V = lambda *s: pltpu.VMEM(s, f)
    return pl.pallas_call(rs_col_kernel, out_shape=jax.ShapeDtypeStruct((S,512), f), in_specs=[VM], out_specs=VM,
        scratch_shapes=[V(2,4,S,256), V(2,2,4,S,256), V(2,4,S,256), V(2,2,4,S,256), V(2,4,S,256), V(2,4,S,256),
            V(2,S,256), V(2,2,S,256), V(2,S,256), V(2,2,S,256), V(2,S,256), V(2,S,256), V(2,S,256),
            pltpu.SemaphoreType.DMA((4,6)), pltpu.SemaphoreType.DMA((4,6)), pltpu.SemaphoreType.DMA((2,)), pltpu.SemaphoreType.DMA((2,))],
        compiler_params=pltpu.CompilerParams(collective_id=cid, has_side_effects=True, vmem_limit_bytes=56*2**20), name="rs_col")(p.reshape(4,2,4,S,512))

class RingAG:
    def __init__(self, part, me, devp, devm, ssem, rsem):
        up = lax.rem(me+1, 4); dn = lax.rem(me+3, 4)
        far = lax.rem(me+2, 4)
        self.s = [rc(part(me,0), part(me,0), ssem.at[0], rsem.at[0], devp),
                  rc(part(me,1), part(me,1), ssem.at[1], rsem.at[1], devm),
                  rc(part(me,1), part(me,1), ssem.at[2], rsem.at[2], devp),
                  rc(part(me,0), part(me,0), ssem.at[3], rsem.at[3], devm),
                  rc(part(dn,0), part(dn,0), ssem.at[4], rsem.at[4], devp),
                  rc(part(up,1), part(up,1), ssem.at[5], rsem.at[5], devm)]
        self.r = [rc(part(dn,0), part(dn,0), ssem.at[0], rsem.at[0], devp),
                  rc(part(up,1), part(up,1), ssem.at[1], rsem.at[1], devm),
                  rc(part(dn,1), part(dn,1), ssem.at[2], rsem.at[2], devp),
                  rc(part(up,0), part(up,0), ssem.at[3], rsem.at[3], devm),
                  rc(part(far,0), part(far,0), ssem.at[4], rsem.at[4], devp),
                  rc(part(far,1), part(far,1), ssem.at[5], rsem.at[5], devm)]
    def start(self):
        for i in range(4): self.s[i].start()
    def forward(self):
        self.r[0].wait_recv(); self.s[4].start()
        self.r[1].wait_recv(); self.s[5].start()
    def finish(self):
        for i in (2,3,4,5): self.r[i].wait_recv()
    def drain(self):
        for i in range(6): self.s[i].wait_send()

def ag_col_kernel(p, o, ss, rs, sx, rx):
    r, y, x, z, dev = place()
    yp, ym = dev(lax.rem(y+1,4),x,z), dev(lax.rem(y+3,4),x,z)
    zp, zm = dev(y,x,lax.rem(z+1,4)), dev(y,x,lax.rem(z+3,4))
    xd = dev(y,1-x,z)
    o[y,x,z] = p[...]
    barrier([yp, ym, zp, zm, xd])
    cx = rc(o.at[y,x,z], o.at[y,x,z], sx.at[0], rx.at[0], xd)
    cxr = rc(o.at[y,1-x,z], o.at[y,1-x,z], sx.at[0], rx.at[0], xd)
    cx.start()
    A = pl.ds(0,256); Bc = pl.ds(256,256)
    cxr.wait_recv()
    a1 = RingAG(lambda k,h: o.at[y,h,k,:,A], z, zp, zm, ss.at[0], rs.at[0])
    b1 = RingAG(lambda k,h: o.at[k,h,z,:,Bc], y, yp, ym, ss.at[1], rs.at[1])
    a1.start(); b1.start()
    a1.forward(); b1.forward()
    a1.finish()
    a2 = RingAG(lambda k,h: o.at[k,h,:,:,A], y, yp, ym, ss.at[2], rs.at[2])
    a2.start()
    b1.finish()
    b2 = RingAG(lambda k,h: o.at[:,h,k,:,Bc], z, zp, zm, ss.at[3], rs.at[3])
    b2.start()
    a2.forward(); b2.forward()
    a2.finish(); b2.finish()
    for t in (a1,b1,a2,b2): t.drain()
    cx.wait_send()

def ag_col(p, cid=2):
    S = 64
    o = pl.pallas_call(ag_col_kernel, out_shape=jax.ShapeDtypeStruct((4,2,4,S,512), jnp.float32), in_specs=[VM], out_specs=VM,
        scratch_shapes=[pltpu.SemaphoreType.DMA((4,6)), pltpu.SemaphoreType.DMA((4,6)), pltpu.SemaphoreType.DMA((1,)), pltpu.SemaphoreType.DMA((1,))],
        compiler_params=pltpu.CompilerParams(collective_id=cid, has_side_effects=True, vmem_limit_bytes=56*2**20), name="ag_col")(p)
    return o.reshape(32*S, 512)

def rs_row_kernel(p, o, rec1, q, rec2, s1, r1, s2, r2):
    r = lax.axis_index("row"); c = lax.axis_index("col")
    h = lax.div(r,2); k = lax.rem(r,2)
    other = (h*2 + 1-k, c); far = ((1-h)*2 + k, c)
    barrier([other, far])
    cs = [rc(p.at[1-h, 1-k], rec1.at[0], s1.at[0], r1.at[0], other), rc(p.at[h, 1-k], rec1.at[1], s1.at[1], r1.at[1], other)]
    for t in cs: t.start()
    cs[0].wait_recv()
    q[...] = p[1-h, k] + rec1[0]
    c2 = rc(q, rec2, s2.at[0], r2.at[0], far); c2.start()
    cs[1].wait_recv()
    o[...] = p[h, k] + rec1[1]
    c2.wait_recv()
    o[...] = o[...] + rec2[...]
    for t in cs: t.wait_send()
    c2.wait_send()

def rs_row(p, cid=3):
    n = p.shape[0]//4
    V = lambda *s: pltpu.VMEM(s, jnp.float32)
    D = pltpu.SemaphoreType.DMA
    return pl.pallas_call(rs_row_kernel, out_shape=jax.ShapeDtypeStruct((n,512), jnp.float32), in_specs=[VM], out_specs=VM,
        scratch_shapes=[V(2,n,512), V(n,512), V(n,512), D((2,)), D((2,)), D((1,)), D((1,))],
        compiler_params=pltpu.CompilerParams(collective_id=cid, has_side_effects=True, vmem_limit_bytes=56*2**20), name="rs_row")(p.reshape(2,2,n,512))

def ag_row_kernel(p, o, s1, r1, s2, r2):
    r = lax.axis_index("row"); c = lax.axis_index("col")
    h = lax.div(r,2); k = lax.rem(r,2)
    other = (h*2 + 1-k, c); far = ((1-h)*2 + k, c)
    o[h, k] = p[...]
    barrier([other, far])
    cf = rc(o.at[h,k], o.at[h,k], s1.at[0], r1.at[0], far)
    cfr = rc(o.at[1-h,k], o.at[1-h,k], s1.at[0], r1.at[0], far)
    cf.start()
    co = rc(o.at[h,k], o.at[h,k], s2.at[0], r2.at[0], other)
    cor = rc(o.at[h,1-k], o.at[h,1-k], s2.at[0], r2.at[0], other)
    co.start()
    cfr.wait_recv()
    co2 = rc(o.at[1-h,k], o.at[1-h,k], s2.at[1], r2.at[1], other)
    co2r = rc(o.at[1-h,1-k], o.at[1-h,1-k], s2.at[1], r2.at[1], other)
    co2.start()
    cor.wait_recv(); co2r.wait_recv()
    cf.wait_send(); co.wait_send(); co2.wait_send()

def ag_row(p, cid=4):
    n = p.shape[0]
    D = pltpu.SemaphoreType.DMA
    o = pl.pallas_call(ag_row_kernel, out_shape=jax.ShapeDtypeStruct((2,2,n,512), jnp.float32), in_specs=[VM], out_specs=VM,
        scratch_shapes=[D((1,)), D((1,)), D((2,)), D((2,))],
        compiler_params=pltpu.CompilerParams(collective_id=cid, has_side_effects=True, vmem_limit_bytes=56*2**20), name="ag_row")(p)
    return o.reshape(4*n, 512)
HI = lax.Precision.HIGHEST
PAIRS = [(i, k) for i in range(4) for k in range(i, 4)]
GROUPS = [(0, 2, "zyx"), (2, 2, "yxz"), (4, 1, "xzy")]

def gram_kernel(s, o, g, crec, *rest):
    bufs, (ssc, rsc, ss, rs) = rest[:-4], rest[-4:]
    r = lax.axis_index("row"); c = lax.axis_index("col")
    xh = lax.div(r, 2); k = lax.rem(r, 2)
    y = lax.div(c, 8); xl = lax.rem(lax.div(c, 4), 2); z = lax.rem(c, 4)
    x = xh*2 + xl
    at = {"x": x, "y": y, "z": z}
    def dev(q):
        return (lax.div(q["x"], 2)*2 + k, q["y"]*8 + lax.rem(q["x"], 2)*4 + q["z"])
    def peer(ax, d):
        q = dict(at); q[ax] = lax.rem(at[ax]+d, 4)
        return q[ax], dev(q)
    other = (xh*2 + 1-k, c)
    barrier([other] + [peer(ax, d)[1] for ax in "xyz" for d in (1,2,3)])
    n = 0
    for i in range(4):
        w = jnp.einsum("ni,nk->ik", s[:, i*128:(i+1)*128], s[:, i*128:], precision=HI, preferred_element_type=jnp.float32)
        for j in range(i, 4):
            g[n//5, n%5] = w[:, (j-i)*128:(j-i+1)*128]
            n += 1
    cc = rc(g.at[1-k], crec, ssc.at[0], rsc.at[0], other)
    cc.start()
    cc.wait_recv()
    g[k] = g[k] + crec[...]
    sends = []
    def exchange(src, buf, ax, sem):
        me = at[ax]
        cs = []
        for d in (1, 3, 2):
            to, dv = peer(ax, d)
            t = rc(src(to), buf.at[me], ss.at[sem, d], rs.at[sem, me], dv)
            t.start(); cs.append(t)
        sends.extend(cs)
        def done():
            for d in (1, 3, 2):
                fr, dv = peer(ax, d)
                rc(src(fr), buf.at[fr], ss.at[sem, d], rs.at[sem, fr], dv).wait_recv()
        return done
    def gather(view, ax, sem):
        me = at[ax]
        cs = []
        for d in (1, 3, 2):
            to, dv = peer(ax, d)
            t = rc(view(me), view(me), ss.at[sem, d], rs.at[sem, me], dv)
            t.start(); cs.append(t)
        sends.extend(cs)
        def done():
            for d in (1, 3, 2):
                fr, dv = peer(ax, d)
                rc(view(fr), view(fr), ss.at[sem, d], rs.at[sem, fr], dv).wait_recv()
        return done
    G3 = range(3)

    b1 = [bufs[3*i] for i in G3]; b2 = [bufs[3*i+1] for i in G3]; b3 = [bufs[3*i+2] for i in G3]
    f = []
    for i, (b0, nb, od) in enumerate(GROUPS):
        f.append(exchange(lambda q, b0=b0, nb=nb: g.at[k, pl.ds(b0, nb), pl.ds(pl.multiple_of(q*32, 32), 32)], b1[i], od[0], i*5))
    for i, (b0, nb, od) in enumerate(GROUPS):
        b1[i][at[od[0]]] = g[k, b0:b0+nb, pl.ds(pl.multiple_of(at[od[0]]*32, 32), 32)]
    f2 = []
    for i, (b0, nb, od) in enumerate(GROUPS):
        f[i]()
        b1[i][4] = (b1[i][0] + b1[i][1]) + (b1[i][2] + b1[i][3])
        f2.append(exchange(lambda q, i=i: b1[i].at[4, :, pl.ds(pl.multiple_of(q*8, 8), 8)], b2[i], od[1], i*5+1))
        b2[i][at[od[1]]] = b1[i][4, :, pl.ds(pl.multiple_of(at[od[1]]*8, 8), 8)]
    f3 = []
    for i, (b0, nb, od) in enumerate(GROUPS):
        f2[i]()
        b3[i][at[od[2]]] = (b2[i][0] + b2[i][1]) + (b2[i][2] + b2[i][3])
        f3.append(gather(lambda q, i=i: b3[i].at[q], od[2], i*5+2))
    f4 = []
    for i, (b0, nb, od) in enumerate(GROUPS):
        f3[i]()
        rows = lambda q, i=i, b0=b0, nb=nb, od=od: o.at[k, pl.ds(b0, nb), pl.ds(pl.multiple_of(at[od[0]]*32 + q*8, 8), 8)]
        rows(at[od[1]])[...] = (b3[i][0] + b3[i][1]) + (b3[i][2] + b3[i][3])
        f4.append(gather(rows, od[1], i*5+3))
    f5 = []
    for i, (b0, nb, od) in enumerate(GROUPS):
        f4[i]()
        f5.append(gather(lambda q, b0=b0, nb=nb: o.at[k, pl.ds(b0, nb), pl.ds(pl.multiple_of(q*32, 32), 32)], od[0], i*5+4))
    for t in f5: t()
    co = rc(o.at[k], o.at[k], ssc.at[1], rsc.at[1], other)
    co.start()
    rc(o.at[1-k], o.at[1-k], ssc.at[1], rsc.at[1], other).wait_recv()
    for t in sends: t.wait_send()
    cc.wait_send(); co.wait_send()

def gram_blocks(s, cid):
    V = lambda *sh: pltpu.VMEM(sh, jnp.float32)
    D = pltpu.SemaphoreType.DMA
    bufs = []
    for b0, nb, od in GROUPS:
        bufs += [V(5, nb, 32, 128), V(4, nb, 8, 128), V(4, nb, 8, 128)]
    return pl.pallas_call(gram_kernel, out_shape=jax.ShapeDtypeStruct((2,5,128,128), jnp.float32), in_specs=[VM], out_specs=VM,
        scratch_shapes=[V(2,5,128,128), V(5,128,128)] + bufs + [D((2,)), D((2,)), D((15,4)), D((15,4))],
        compiler_params=pltpu.CompilerParams(collective_id=cid, has_side_effects=True, vmem_limit_bytes=56*2**20), name="gram")(s)
HI = lax.Precision.HIGHEST
B = 128

def mm(a, b):
    return jnp.dot(a, b, precision=HI, preferred_element_type=jnp.float32)

def leaf_inverse(a):
    n = B // 8
    lane = lax.broadcasted_iota(jnp.int32, (1, B), 1)
    sub = lax.broadcasted_iota(jnp.int32, (8, B), 0)
    lane8 = lax.broadcasted_iota(jnp.int32, (8, B), 1)
    ch = [a[8*t:8*t+8, :] for t in range(n)]
    drow = jnp.zeros((8, B), jnp.float32)
    for t in range(n):
        drow = drow + jnp.where(lane8 == sub + 8*t, ch[t], 0.0)
    srow = lax.rsqrt(jnp.sum(drow, axis=0, keepdims=True))
    srow8 = jnp.broadcast_to(srow, (8, B))
    for t in range(n):
        scol = jnp.sum(jnp.where(lane8 == sub + 8*t, srow8, 0.0), axis=1, keepdims=True)
        ch[t] = ch[t] * srow8 * scol
    for j in range(0, B, 4):
        t0, s = divmod(j, 8)
        c = [jnp.broadcast_to(ch[t0][:, j+b:j+b+1], (8, B)) for b in range(4)]
        pv = lambda i, k: c[k][s+i:s+i+1]
        piv = [lane == j+b for b in range(4)]
        inpiv = (lane >= j) & (lane < j+4)
        R = [jnp.where(piv[b], 1.0, jnp.where(inpiv, 0.0, ch[t0][s+b:s+b+1, :])) for b in range(4)]
        p, q, d = pv(0, 0), pv(1, 0), pv(1, 1)
        det = p*d - q*q
        idet = 1.0 / det
        ip, iq, iD = d*idet, -q*idet, p*idet
        t00 = pv(2,0)*ip + pv(2,1)*iq; t01 = pv(2,0)*iq + pv(2,1)*iD
        t10 = pv(3,0)*ip + pv(3,1)*iq; t11 = pv(3,0)*iq + pv(3,1)*iD
        s00 = pv(2,2) - (t00*pv(2,0) + t01*pv(2,1))
        s10 = pv(3,2) - (t10*pv(2,0) + t11*pv(2,1))
        s11 = pv(3,3) - (t10*pv(3,0) + t11*pv(3,1))
        dets = s00*s11 - s10*s10
        idets = 1.0 / dets
        v0 = R[2] - (t00*R[0] + t01*R[1])
        v1 = R[3] - (t10*R[0] + t11*R[1])
        w2 = (s11*v0 - s10*v1) * idets
        w3 = (s00*v1 - s10*v0) * idets
        w0 = (ip*R[0] + iq*R[1]) - (t00*w2 + t10*w3)
        w1 = (iq*R[0] + iD*R[1]) - (t01*w2 + t11*w3)
        W = [jnp.broadcast_to(w, (8, B)) for w in (w0, w1, w2, w3)]
        ipp = 1.0 / p; iss = 1.0 / s00
        F = [R[0]*lax.rsqrt(p), (R[1] - (q*ipp)*R[0])*lax.rsqrt(det*ipp), v0*lax.rsqrt(s00), (v1 - (s10*iss)*v0)*lax.rsqrt(dets*iss)]
        inpiv8 = (lane8 >= j) & (lane8 < j+4)
        for t in range(t0, n):
            if t == t0:
                m = [jnp.where(sub > s+3, c[b], 0.0) for b in range(4)]
            else:
                m = [jnp.broadcast_to(ch[t][:, j+b:j+b+1], (8, B)) for b in range(4)]
            u = (m[0]*W[0] + m[1]*W[1]) + (m[2]*W[2] + m[3]*W[3])
            ch[t] = jnp.where(inpiv8, 0.0, ch[t]) - u
            if t == t0:
                for b in range(4):
                    ch[t] = jnp.where(sub == s+b, jnp.broadcast_to(jnp.where(lane <= j+b, F[b], 0.0), (8, B)), ch[t])

    return jnp.concatenate([x * srow8 for x in ch], 0)

def chol_kernel(g_ref, x_ref):
    n = 0
    for i in range(4):
        for k in range(4):
            if k >= i:
                x_ref[i*B:(i+1)*B, k*B:(k+1)*B] = g_ref[n]
                n += 1
            else:
                x_ref[i*B:(i+1)*B, k*B:(k+1)*B] = jnp.zeros((B, B), jnp.float32)
    for J in range(4):
        lo, hi = J*B, (J+1)*B
        x = leaf_inverse(x_ref[lo:hi, lo:hi])
        x_ref[lo:hi, lo:hi] = x
        if J > 0:
            x_ref[lo:hi, 0:lo] = mm(x, x_ref[lo:hi, 0:lo])
        if J < 3:
            right = mm(x, x_ref[lo:hi, hi:])
            rt = right.T
            x_ref[lo:hi, hi:] = right
            x_ref[hi:, hi:] = x_ref[hi:, hi:] - mm(rt, right)
            left = mm(rt, x_ref[lo:hi, 0:hi])
            if J > 0:
                x_ref[hi:, 0:lo] = x_ref[hi:, 0:lo] - left[:, 0:lo]
            x_ref[hi:, lo:hi] = -left[:, lo:hi]
            x_ref[lo:hi, hi:] = jnp.zeros_like(right)

def chol_inverse(g):
    return pl.pallas_call(chol_kernel, out_shape=jax.ShapeDtypeStruct((4*B, 4*B), jnp.float32),
        in_specs=[pl.BlockSpec(memory_space=pltpu.VMEM)], out_specs=pl.BlockSpec(memory_space=pltpu.VMEM),
        compiler_params=pltpu.CompilerParams(vmem_limit_bytes=48*2**20), name="chol")(g)
M = 8192


def apply_inverse(rows, x):
    return lax.dot_general(rows, x, (((1,), (1,)), ((), ())), precision=HI, preferred_element_type=jnp.float32)


def shards(adjusted_weight, base_weight, test_matrix):
    delta = adjusted_weight.astype(jnp.float32) - base_weight.astype(jnp.float32)
    scale_out = jnp.sqrt(jnp.float32(M))
    own = rs_col(mm(delta, test_matrix))
    x1 = chol_inverse(gram_blocks(own, 5).reshape(10, B, B))
    sketch = ag_col(own)
    raw = rs_row(jnp.einsum("mn,mk->nk", delta, sketch, precision=HI, preferred_element_type=jnp.float32))
    own_co = apply_inverse(raw, x1)
    x2 = chol_inverse(gram_blocks(own_co, 6).reshape(10, B, B))
    cosketch = ag_row(own_co)
    own = apply_inverse(rs_col(mm(delta, cosketch)), x2)
    x3 = chol_inverse(gram_blocks(own, 5).reshape(10, B, B))
    return scale_out * apply_inverse(own, x3)


def solution(mesh):
    return jax.shard_map(
        shards,
        mesh=mesh,
        in_specs=(P("row", "col"), P("row", "col"), P("col", None)),
        out_specs=P(("row", "col"), None),
        check_vma=False,
    )
```

time: 1780 us -> 449 us (0.25)
  waiting for transfers between devices: 1170 us -> 0 us
  other arithmetic: 371 us -> 13.7 us
  Pallas kernels: 0 us -> 317 us
  matrix products: 172 us -> 93.6 us
  local copies, waits for them, and re-layouts: 40.5 us -> 17.8 us
  between operations: 22 us -> 0.57 us
    psum x6 -> x0, waiting for transfers between devices: 1170 us -> none  [the longest x2 602 us: column_sum(): return lax.psum(partial_sketch, 'col')]
    another operation x51 -> x0, other arithmetic: 366 us -> none  [the longest x44 243 us: gram_factor(): return jnp.linalg.cholesky(summed)]
    pallas_call x0 -> x11, Pallas kernels: none -> 317 us  [the longest x3 84.8 us: gram_blocks(): pl.pallas_call(gram_kernel, out_shape=jax.ShapeDtypeStruct((2, 5, 128, 12...]
    another operation x39 -> x0, matrix products: 60.8 us -> none  [the longest x21 47.5 us: apply_inverse(): lax.linalg.triangular_solve(factor_low, sketch_rows, left_side=False, low...]
    another operation x49 -> x0, local copies, waits for them, and re-layouts: 31.4 us -> none
    dot_general x6, matrix products: 111 us -> 93.6 us  [the longest x2 56.3 us: mm(): return jnp.dot(a, b, precision=HI, preferred_element_type=jnp.float32)]
  transfers between devices with their start and end apart: 6 -> 0, of which waited for: 6 -> 0; matrix products, arithmetic and copies ran while one was open for 0% -> 0% of each run, Pallas kernels for 0% -> 0%
where the time goes in v1:
time: 449 us; the launch traced here: 443 us
  Pallas kernels  317 us (71%)
  matrix products  93.6 us (21%)
  local copies, waits for them, and re-layouts  17.8 us (4%)
  other arithmetic  13.7 us (3%)
    pallas_call x3, Pallas kernels, gram_blocks(): pl.pallas_call(gram_kernel, out_shape=jax.ShapeDtypeStruct((2, 5, 128, 12...  84.8 us
    pallas_call x3, Pallas kernels, chol_inverse(): pl.pallas_call(chol_kernel, out_shape=jax.ShapeDtypeStruct((4 * B, 4 * B)...  71.6 us
    pallas_call x2, Pallas kernels, rs_col(): pl.pallas_call(rs_col_kernel, out_shape=jax.ShapeDtypeStruct((S, 512), f)...  69.4 us
    dot_general x2, matrix products, mm(): return jnp.dot(a, b, precision=HI, preferred_element_type=jnp.float32)  56.3 us
    pallas_call x1, Pallas kernels, rs_row(): pl.pallas_call(rs_row_kernel, out_shape=jax.ShapeDtypeStruct((n, 512), jn...  35.3 us
    pallas_call x1, Pallas kernels, ag_col(): pl.pallas_call(ag_col_kernel, out_shape=jax.ShapeDtypeStruct((4, 2, 4, S,...  28.5 us
    dot_general x1, matrix products, shards(): jnp.einsum('mn,mk->nk', delta, sketch, precision=HI, preferred_element_ty...  28.3 us
    pallas_call x1, Pallas kernels, ag_row(): pl.pallas_call(ag_row_kernel, out_shape=jax.ShapeDtypeStruct((2, 2, n, 51...  27.7 us

profile of v1, /device:TPU:1, one launch (start us, length us, event | category | flops | bytes accessed | tf_op | source)
XLA Modules:
  0.0 442.9 jit_solution(10205421361347115599)
XLA Ops:
  0.0 13.7 %fusion.1 = (f32[1664,2048]{0,1:T(8,128)}, f32[2048,1664]{1,0:T(8,128)}) fusion(bf16[2048,1664]{1,0:T(8,128)(2,1)} %param.4, bf16[2048,1664]{1,0:T(8,128)(2,1)} %param.3), kind=kLoop, calls=%fused_computation.3 | loop fusion | flops 10223616 | bytes 40894464 | tf_op jit(solution)/shard_map/mn,mk->nk/dot_general | solution.py:409
  13.7 14.5 %copy.6 = f32[1664,2048]{1,0:T(8,128)} copy(f32[1664,2048]{0,1:T(8,128)} %get-tuple-element.5) | data formatting | bytes 27262976 | tf_op jit(solution)/shard_map/mn,mk->nk/dot_general | solution.py:409
  28.3 27.5 %fusion = f32[2048,512]{1,0:T(8,128)} fusion(f32[1664,512]{1,0:T(8,128)S(1)} %copy-done, bf16[2048,1664]{1,0:T(8,128)(2,1)} %param.4, bf16[2048,1664]{1,0:T(8,128)(2,1)} %param.3), kind=kOutput, calls=%fused_computation.2 | convolution fusion | flops 20948189184 | bytes 21233664 | tf_op jit(solution)/shard_map/dot_general | solution.py:309
  55.8 36.9 %rs_col.2.p.s = f32[64,512]{1,0:T(8,128)} custom-call(f32[4,2,4,64,512]{4,3,2,1,0:T(8,128)} %bitcast.35), custom_call_target="tpu_custom_call" | custom-call | tf_op jit(solution)/shard_map/rs_col/pallas_call | solution.py:88
  92.7 28.5 %ag_col.1 = f32[4,2,4,64,512]{4,3,2,1,0:T(8,128)} custom-call(f32[64,512]{1,0:T(8,128)} %rs_col.2.p.s), custom_call_target="tpu_custom_call" | custom-call | tf_op jit(solution)/shard_map/ag_col/pallas_call | solution.py:149
  121.2 28.3 %fusion.2.p = f32[2,2,416,512]{3,2,1,0:T(8,128)} fusion(f32[2,2,416,2048]{3,2,1,0:T(8,128)} %bitcast.33, f32[2048,512,1,1]{1,0,3,2:T(8,128)} %bitcast.34), kind=kOutput, calls=%fused_computation.4 | convolution fusion | flops 20937965568 | bytes 21233664 | tf_op jit(solution)/shard_map/mn,mk->nk/dot_general | solution.py:409
  149.5 35.3 %rs_row.1 = f32[416,512]{1,0:T(8,128)} custom-call(f32[2,2,416,512]{3,2,1,0:T(8,128)} %fusion.2.p), custom_call_target="tpu_custom_call" | custom-call | tf_op jit(solution)/shard_map/rs_row/pallas_call | solution.py:175
  184.8 27.2 %gram.3 = f32[2,5,128,128]{3,2,1,0:T(8,128)} custom-call(f32[64,512]{1,0:T(8,128)} %rs_col.2.p.s), custom_call_target="tpu_custom_call" | custom-call | tf_op jit(solution)/shard_map/gram/pallas_call | solution.py:302
  212.0 1.1 copy-done.2
  213.1 24.0 %chol.3 = f32[512,512]{1,0:T(8,128)S(1)} custom-call(f32[10,128,128]{2,1,0:T(8,128)S(1)} %bitcast.29), custom_call_target="tpu_custom_call" | custom-call | tf_op jit(solution)/shard_map/chol/pallas_call | solution.py:393
  237.1 3.6 fusion.3.p.s
  240.7 27.7 %ag_row.1 = f32[2,2,416,512]{3,2,1,0:T(8,128)} custom-call(f32[416,512]{1,0:T(8,128)} %fusion.3.p.s), custom_call_target="tpu_custom_call" | custom-call | tf_op jit(solution)/shard_map/ag_row/pallas_call | solution.py:201
  268.5 0.0 copy-start.1
  268.5 28.8 %fusion.4.p = f32[4,2,4,64,512]{4,3,2,1,0:T(8,128)} fusion(f32[4,2,4,64,1664]{4,3,2,1,0:T(8,128)} %bitcast.32, f32[1664,512,1,1,1]{1,0,4,3,2:T(8,128)} %bitcast.36), kind=kOutput, calls=%fused_computation.6 | convolution fusion | flops 20937965568 | bytes 21233664 | tf_op jit(solution)/shard_map/dot_general | solution.py:309
  297.2 32.5 %rs_col.3 = f32[64,512]{1,0:T(8,128)} custom-call(f32[4,2,4,64,512]{4,3,2,1,0:T(8,128)} %fusion.4.p), custom_call_target="tpu_custom_call" | custom-call | tf_op jit(solution)/shard_map/rs_col/pallas_call | solution.py:88
  329.7 30.5 %gram.4 = f32[2,5,128,128]{3,2,1,0:T(8,128)} custom-call(f32[416,512]{1,0:T(8,128)} %fusion.3.p.s), custom_call_target="tpu_custom_call" | custom-call | tf_op jit(solution)/shard_map/gram/pallas_call | solution.py:302
  360.3 1.1 copy-done.3
  361.4 23.8 %chol.4 = f32[512,512]{1,0:T(8,128)S(1)} custom-call(f32[10,128,128]{2,1,0:T(8,128)S(1)} %bitcast.30), custom_call_target="tpu_custom_call" | custom-call | tf_op jit(solution)/shard_map/chol/pallas_call | solution.py:393
  385.1 2.7 fusion.5.s
  387.8 27.1 %gram.5 = f32[2,5,128,128]{3,2,1,0:T(8,128)} custom-call(f32[64,512]{1,0:T(8,128)} %fusion.5.s), custom_call_target="tpu_custom_call" | custom-call | tf_op jit(solution)/shard_map/gram/pallas_call | solution.py:302
  414.9 1.1 copy-done.4
  416.0 23.8 %chol.5 = f32[512,512]{1,0:T(8,128)S(1)} custom-call(f32[10,128,128]{2,1,0:T(8,128)S(1)} %bitcast.31), custom_call_target="tpu_custom_call" | custom-call | tf_op jit(solution)/shard_map/chol/pallas_call | solution.py:393
  439.8 2.7 convolution_multiply_fusion
  442.5 0.0 copy-done.1
  (5 shorter events, 0.0 us)
Async XLA Ops:
  0.0 28.3 %copy-start = (f32[1664,512]{1,0:T(8,128)S(1)}, f32[1664,512]{1,0:T(8,128)}, u32[]{:S(2)}) copy-start(f32[1664,512]{1,0:T(8,128)} %param.5) | copy-start | bytes 10223620
  212.0 1.1 copy-start.2
  268.5 174.0 %copy-start.1 = (f32[1664,512]{1,0:T(8,128)S(1)}, f32[1664,512]{1,0:T(8,128)}, u32[]{:S(2)}) copy-start(f32[1664,512]{1,0:T(8,128)} %param.5) | copy-start | bytes 10223620
  360.3 1.1 copy-start.3
  414.9 1.1 copy-start.4

commit v2 on v1

--- a/solution.py
+++ b/solution.py
@@ -393,26 +393,372 @@
     return pl.pallas_call(chol_kernel, out_shape=jax.ShapeDtypeStruct((4*B, 4*B), jnp.float32),
         in_specs=[pl.BlockSpec(memory_space=pltpu.VMEM)], out_specs=pl.BlockSpec(memory_space=pltpu.VMEM),
         compiler_params=pltpu.CompilerParams(vmem_limit_bytes=48*2**20), name="chol")(g)
-M = 8192
-
-
-def apply_inverse(rows, x):
+
+def chol_load(g, x_ref):
+    n = 0
+    for i in range(4):
+        for k in range(4):
+            if k >= i:
+                x_ref[i*B:(i+1)*B, k*B:(k+1)*B] = g[n]
+                n += 1
+            else:
+                x_ref[i*B:(i+1)*B, k*B:(k+1)*B] = jnp.zeros((B, B), jnp.float32)
+
+def chol_steps(g, x_ref):
+    chol_load(g, x_ref)
+    for J in range(4):
+        lo, hi = J*B, (J+1)*B
+        x = leaf_inverse(x_ref[lo:hi, lo:hi])
+        x_ref[lo:hi, lo:hi] = x
+        if J > 0:
+            x_ref[lo:hi, 0:lo] = mm(x, x_ref[lo:hi, 0:lo])
+        if J < 3:
+            right = mm(x, x_ref[lo:hi, hi:])
+            rt = right.T
+            x_ref[lo:hi, hi:] = right
+            x_ref[hi:, hi:] = x_ref[hi:, hi:] - mm(rt, right)
+            left = mm(rt, x_ref[lo:hi, 0:hi])
+            if J > 0:
+                x_ref[hi:, 0:lo] = x_ref[hi:, 0:lo] - left[:, 0:lo]
+            x_ref[hi:, lo:hi] = -left[:, lo:hi]
+            x_ref[lo:hi, hi:] = jnp.zeros_like(right)
+        yield
+
+def run(gen):
+    for _ in gen:
+        pass
+
+def alternate(first, *others):
+    gens = [first, *others]
+    while gens:
+        for t in list(gens):
+            try:
+                next(t)
+            except StopIteration:
+                gens.remove(t)
+
+def mesh_place():
+    r = lax.axis_index("row"); c = lax.axis_index("col")
+    q = {"xh": lax.div(r, 2), "core": lax.rem(r, 2), "y": lax.div(c, 8), "xl": lax.rem(lax.div(c, 4), 2), "z": lax.rem(c, 4)}
+    q["x"] = q["xh"]*2 + q["xl"]
+    return r, c, q
+
+def col_neighbours(r, q):
+    def dev(y, x, z):
+        return (r, y*8 + x*4 + z)
+    y, x, z = q["y"], q["xl"], q["z"]
+    return {"yp": dev(lax.rem(y+1,4),x,z), "ym": dev(lax.rem(y+3,4),x,z), "zp": dev(y,x,lax.rem(z+1,4)), "zm": dev(y,x,lax.rem(z+3,4)), "xd": dev(y,1-x,z)}
+
+def row_neighbours(c, q):
+    h, k = q["xh"], q["core"]
+    return {"other": (h*2 + 1-k, c), "far": ((1-h)*2 + k, c)}
+
+def axis_peer(q, ax, d):
+    t = dict(q); t[ax] = lax.rem(q[ax]+d, 4)
+    return t[ax], (lax.div(t["x"], 2)*2 + t["core"], t["y"]*8 + lax.rem(t["x"], 2)*4 + t["z"])
+
+def gram_devices(c, q):
+    return [row_neighbours(c, q)["other"]] + [axis_peer(q, ax, d)[1] for ax in "xyz" for d in (1, 2, 3)]
+
+def gram_scratch():
+    V = lambda *sh: pltpu.VMEM(sh, jnp.float32)
+    D = pltpu.SemaphoreType.DMA
+    bufs = [V(2,5,128,128), V(5,128,128)]
+    for b0, nb, od in GROUPS:
+        bufs += [V(5, nb, 32, 128), V(4, nb, 8, 128), V(4, nb, 8, 128)]
+    return bufs + [D((2,)), D((2,)), D((15,4)), D((15,4))]
+NGRAM = 15
+
+def gram_steps(s, o, c, q, scr):
+    g, crec, bufs, (ssc, rsc, ss, rs) = scr[0], scr[1], scr[2:11], scr[11:]
+    k = q["core"]; at = q
+    other = row_neighbours(c, q)["other"]
+    n = 0
+    for i in range(4):
+        w = jnp.einsum("ni,nk->ik", s[:, i*128:(i+1)*128], s[:, i*128:], precision=HI, preferred_element_type=jnp.float32)
+        for j in range(i, 4):
+            g[n//5, n%5] = w[:, (j-i)*128:(j-i+1)*128]
+            n += 1
+    cc = rc(g.at[1-k], crec, ssc.at[0], rsc.at[0], other)
+    cc.start()
+    yield
+    cc.wait_recv()
+    g[k] = g[k] + crec[...]
+    sends = []
+    def exchange(src, buf, ax, sem):
+        me = at[ax]
+        for d in (1, 3, 2):
+            to, dv = axis_peer(q, ax, d)
+            t = rc(src(to), buf.at[me], ss.at[sem, d], rs.at[sem, me], dv)
+            t.start(); sends.append(t)
+        def done():
+            for d in (1, 3, 2):
+                fr, dv = axis_peer(q, ax, d)
+                rc(src(fr), buf.at[fr], ss.at[sem, d], rs.at[sem, fr], dv).wait_recv()
+        return done
+    def gather(view, ax, sem):
+        me = at[ax]
+        for d in (1, 3, 2):
+            to, dv = axis_peer(q, ax, d)
+            t = rc(view(me), view(me), ss.at[sem, d], rs.at[sem, me], dv)
+            t.start(); sends.append(t)
+        def done():
+            for d in (1, 3, 2):
+                fr, dv = axis_peer(q, ax, d)
+                rc(view(fr), view(fr), ss.at[sem, d], rs.at[sem, fr], dv).wait_recv()
+        return done
+    b1 = [bufs[3*i] for i in range(3)]; b2 = [bufs[3*i+1] for i in range(3)]; b3 = [bufs[3*i+2] for i in range(3)]
+    m32 = lambda i: pl.ds(pl.multiple_of(i*32, 32), 32)
+    m8 = lambda i: pl.ds(pl.multiple_of(i*8, 8), 8)
+    f = []
+    for i, (b0, nb, od) in enumerate(GROUPS):
+        f.append(exchange(lambda t, b0=b0, nb=nb: g.at[k, pl.ds(b0, nb), m32(t)], b1[i], od[0], i*5))
+    for i, (b0, nb, od) in enumerate(GROUPS):
+        b1[i][at[od[0]]] = g[k, b0:b0+nb, m32(at[od[0]])]
+    yield
+    f2 = []
+    for i, (b0, nb, od) in enumerate(GROUPS):
+        f[i]()
+        b1[i][4] = (b1[i][0] + b1[i][1]) + (b1[i][2] + b1[i][3])
+        f2.append(exchange(lambda t, i=i: b1[i].at[4, :, m8(t)], b2[i], od[1], i*5+1))
+        b2[i][at[od[1]]] = b1[i][4, :, m8(at[od[1]])]
+    yield
+    f3 = []
+    for i, (b0, nb, od) in enumerate(GROUPS):
+        f2[i]()
+        b3[i][at[od[2]]] = (b2[i][0] + b2[i][1]) + (b2[i][2] + b2[i][3])
+        f3.append(gather(lambda t, i=i: b3[i].at[t], od[2], i*5+2))
+    yield
+    f4 = []
+    for i, (b0, nb, od) in enumerate(GROUPS):
+        f3[i]()
+        rows = lambda t, b0=b0, nb=nb, od=od: o.at[k, pl.ds(b0, nb), pl.ds(pl.multiple_of(at[od[0]]*32 + t*8, 8), 8)]
+        rows(at[od[1]])[...] = (b3[i][0] + b3[i][1]) + (b3[i][2] + b3[i][3])
+        f4.append(gather(rows, od[1], i*5+3))
+    yield
+    f5 = []
+    for i, (b0, nb, od) in enumerate(GROUPS):
+        f4[i]()
+        f5.append(gather(lambda t, b0=b0, nb=nb: o.at[k, pl.ds(b0, nb), m32(t)], od[0], i*5+4))
+    yield
+    for t in f5: t()
+    co = rc(o.at[k], o.at[k], ssc.at[1], rsc.at[1], other)
+    co.start()
+    yield
+    rc(o.at[1-k], o.at[1-k], ssc.at[1], rsc.at[1], other).wait_recv()
+    for t in sends: t.wait_send()
+    cc.wait_send(); co.wait_send()
+
+A = pl.ds(0, 256); Bc = pl.ds(256, 256)
+
+def rs_scratch():
+    S = 64
+    V = lambda *s: pltpu.VMEM(s, jnp.float32)
+    D = pltpu.SemaphoreType.DMA
+    return [V(2,4,S,256), V(2,2,4,S,256), V(2,4,S,256), V(2,2,4,S,256), V(2,4,S,256), V(2,4,S,256),
+            V(2,S,256), V(2,2,S,256), V(2,S,256), V(2,2,S,256), V(2,S,256), V(2,S,256), V(2,S,256),
+            D((4,6)), D((4,6)), D((2,)), D((2,))]
+
+def rs_steps(p, o, q, nb, scr):
+    relA, finA, relB, finB, qa, qb, relA2, finA2, relB2, finB2, ra, rb, recx, ss, rs, sx, rx = scr
+    y, x, z = q["y"], q["xl"], q["z"]
+    yp, ym, zp, zm, xd = nb["yp"], nb["ym"], nb["zp"], nb["zm"], nb["xd"]
+    a1 = RingRS(lambda k,h: p.at[k,h,:,:,A], y, yp, ym, relA, finA, ss.at[0], rs.at[0])
+    b1 = RingRS(lambda k,h: p.at[:,h,k,:,Bc], z, zp, zm, relB, finB, ss.at[1], rs.at[1])
+    a1.start(); b1.start()
+    yield
+    a1.forward(); b1.forward()
+    yield
+    a1.finish(qa)
+    a2 = RingRS(lambda k,h: qa.at[h,k], z, zp, zm, relA2, finA2, ss.at[2], rs.at[2])
+    a2.start()
+    b1.finish(qb)
+    b2 = RingRS(lambda k,h: qb.at[h,k], y, yp, ym, relB2, finB2, ss.at[3], rs.at[3])
+    b2.start()
+    a2.forward(); b2.forward()
+    yield
+    a2.finish(ra)
+    cxa = rc(ra.at[1-x], recx.at[0], sx.at[0], rx.at[0], xd); cxa.start()
+    b2.finish(rb)
+    cxb = rc(rb.at[1-x], recx.at[1], sx.at[1], rx.at[1], xd); cxb.start()
+    cxa.wait_recv()
+    o[:, 0:256] = ra[x] + recx[0]
+    cxb.wait_recv()
+    o[:, 256:512] = rb[x] + recx[1]
+    for t in (a1, b1, a2, b2): t.drain()
+    cxa.wait_send(); cxb.wait_send()
+
+def ag_scratch():
+    D = pltpu.SemaphoreType.DMA
+    return [D((4,6)), D((4,6)), D((1,)), D((1,))]
+
+def ag_steps(o, q, nb, scr):
+    ss, rs, sx, rx = scr
+    y, x, z = q["y"], q["xl"], q["z"]
+    yp, ym, zp, zm, xd = nb["yp"], nb["ym"], nb["zp"], nb["zm"], nb["xd"]
+    cx = rc(o.at[y,x,z], o.at[y,x,z], sx.at[0], rx.at[0], xd)
+    cxr = rc(o.at[y,1-x,z], o.at[y,1-x,z], sx.at[0], rx.at[0], xd)
+    cx.start()
+    yield
+    cxr.wait_recv()
+    a1 = RingAG(lambda k,h: o.at[y,h,k,:,A], z, zp, zm, ss.at[0], rs.at[0])
+    b1 = RingAG(lambda k,h: o.at[k,h,z,:,Bc], y, yp, ym, ss.at[1], rs.at[1])
+    a1.start(); b1.start()
+    yield
+    a1.forward(); b1.forward()
+    yield
+    a1.finish()
+    a2 = RingAG(lambda k,h: o.at[k,h,:,:,A], y, yp, ym, ss.at[2], rs.at[2])
+    a2.start()
+    b1.finish()
+    b2 = RingAG(lambda k,h: o.at[:,h,k,:,Bc], z, zp, zm, ss.at[3], rs.at[3])
+    b2.start()
+    yield
+    a2.forward(); b2.forward()
+    yield
+    a2.finish(); b2.finish()
+    for t in (a1,b1,a2,b2): t.drain()
+    cx.wait_send()
+
+def row_rs_scratch(n):
+    V = lambda *s: pltpu.VMEM(s, jnp.float32)
+    D = pltpu.SemaphoreType.DMA
+    return [V(2,n,512), V(n,512), V(n,512), D((2,)), D((2,)), D((1,)), D((1,))]
+
+def row_rs_steps(p, o, q, nb, scr):
+    rec1, qf, rec2, s1, r1, s2, r2 = scr
+    h, k = q["xh"], q["core"]
+    cs = [rc(p.at[1-h, 1-k], rec1.at[0], s1.at[0], r1.at[0], nb["other"]), rc(p.at[h, 1-k], rec1.at[1], s1.at[1], r1.at[1], nb["other"])]
+    for t in cs: t.start()
+    cs[0].wait_recv()
+    qf[...] = p[1-h, k] + rec1[0]
+    c2 = rc(qf, rec2, s2.at[0], r2.at[0], nb["far"]); c2.start()
+    cs[1].wait_recv()
+    o[...] = p[h, k] + rec1[1]
+    yield
+    c2.wait_recv()
+    o[...] = o[...] + rec2[...]
+    for t in cs: t.wait_send()
+    c2.wait_send()
+
+def row_ag_scratch():
+    D = pltpu.SemaphoreType.DMA
+    return [D((1,)), D((1,)), D((2,)), D((2,))]
+
+def row_ag_steps(o, q, nb, scr):
+    s1, r1, s2, r2 = scr
+    h, k = q["xh"], q["core"]
+    cf = rc(o.at[h,k], o.at[h,k], s1.at[0], r1.at[0], nb["far"])
+    cfr = rc(o.at[1-h,k], o.at[1-h,k], s1.at[0], r1.at[0], nb["far"])
+    cf.start()
+    co = rc(o.at[h,k], o.at[h,k], s2.at[0], r2.at[0], nb["other"])
+    cor = rc(o.at[h,1-k], o.at[h,1-k], s2.at[0], r2.at[0], nb["other"])
+    co.start()
+    yield
+    cor.wait_recv()
+    yield
+    cfr.wait_recv()
+    co2 = rc(o.at[1-h,k], o.at[1-h,k], s2.at[1], r2.at[1], nb["other"])
+    co2r = rc(o.at[1-h,1-k], o.at[1-h,1-k], s2.at[1], r2.at[1], nb["other"])
+    co2.start()
+    yield
+    co2r.wait_recv()
+    cf.wait_send(); co.wait_send(); co2.wait_send()
+
+
+def call(kernel, name, cid, outs, scratch, *args):
+    return pl.pallas_call(kernel, out_shape=[jax.ShapeDtypeStruct(s, jnp.float32) for s in outs],
+        in_specs=[VM]*len(args), out_specs=[VM]*len(outs), scratch_shapes=scratch,
+        compiler_params=pltpu.CompilerParams(collective_id=cid, has_side_effects=True, vmem_limit_bytes=60*2**20), name=name)(*args)
+
+def gather_gram_kernel(p, o, gb, *scr):
+    r, c, q = mesh_place()
+    nb = col_neighbours(r, q)
+    o[q["y"], q["xl"], q["z"]] = p[...]
+    barrier(list(nb.values()) + gram_devices(c, q))
+    alternate(ag_steps(o, q, nb, scr[NGRAM:]), gram_steps(p, gb, c, q, scr[:NGRAM]))
+
+def gather_gram(own):
+    o, g = call(gather_gram_kernel, "gather_gram", 1, [(4,2,4,64,512), (2,5,B,B)], gram_scratch() + ag_scratch(), own)
+    return o.reshape(2048, 512), g
+
+def row_sum_chol_kernel(p, g, o, x, *scr):
+    r, c, q = mesh_place()
+    nb = row_neighbours(c, q)
+    barrier(list(nb.values()))
+    alternate(row_rs_steps(p, o, q, nb, scr), chol_steps_once(g, x))
+
+def chol_steps_once(g, x):
+    run(chol_steps(g, x))
+    yield
+
+def row_sum_chol(w, g):
+    n = w.shape[0]//4
+    return call(row_sum_chol_kernel, "row_sum_chol", 2, [(n, 512), (512, 512)], row_rs_scratch(n), w.reshape(2,2,n,512), g.reshape(10,B,B))
+
+def apply_t(rows, x):
     return lax.dot_general(rows, x, (((1,), (1,)), ((), ())), precision=HI, preferred_element_type=jnp.float32)
 
-
+def norm_gather_kernel(p, x, o, gb, own, *scr):
+    r, c, q = mesh_place()
+    nb = row_neighbours(c, q)
+    own[...] = apply_t(p[...], x[...])
+    o[q["xh"], q["core"]] = own[...]
+    barrier([nb["far"]] + gram_devices(c, q))
+    alternate(row_ag_steps(o, q, nb, scr[NGRAM:]), gram_steps(own, gb, c, q, scr[:NGRAM]))
+
+def norm_gather(raw, x):
+    n = raw.shape[0]
+    o, g = call(norm_gather_kernel, "norm_gather", 3, [(2,2,n,512), (2,5,B,B)], [pltpu.VMEM((n,512), jnp.float32)] + gram_scratch() + row_ag_scratch(), raw, x)
+    return o.reshape(4*n, 512), g
+
+def col_sum_kernel(p, o, *scr):
+    r, c, q = mesh_place()
+    nb = col_neighbours(r, q)
+    barrier(list(nb.values()))
+    run(rs_steps(p, o, q, nb, scr))
+
+def col_sum(p):
+    return call(col_sum_kernel, "col_sum", 4, [(64,512)], rs_scratch(), p.reshape(4,2,4,64,512))[0]
+
+def col_sum_chol_kernel(p, g, o, x, *scr):
+    r, c, q = mesh_place()
+    nb = col_neighbours(r, q)
+    barrier(list(nb.values()))
+    rsg = rs_steps(p, o, q, nb, scr); ch = chol_steps(g, x)
+    next(rsg); next(ch)
+    next(rsg); next(ch); next(ch)
+    next(rsg); next(ch)
+    run(rsg); run(ch)
+
+def col_sum_chol(p, g):
+    return call(col_sum_chol_kernel, "col_sum_chol", 5, [(64,512), (512,512)], rs_scratch(), p.reshape(4,2,4,64,512), g.reshape(10,B,B))
+
+def last_kernel(p, x2, o, own, gb, x3, *scr):
+    r, c, q = mesh_place()
+    own[...] = apply_t(p[...], x2[...])
+    barrier(gram_devices(c, q))
+    run(gram_steps(own, gb, c, q, scr))
+    run(chol_steps(Blocks(gb), x3))
+    o[...] = SCALE * apply_t(own[...], x3[...])
+
+class Blocks:
+    def __init__(self, ref): self.ref = ref
+    def __getitem__(self, n): return self.ref[n//5, n%5]
+
+SCALE = float(8192.0 ** 0.5)
+
+def last(raw, x2):
+    V = lambda *s: pltpu.VMEM(s, jnp.float32)
+    return call(last_kernel, "last", 6, [(64,512)], [V(64,512), V(2,5,B,B), V(512,512)] + gram_scratch(), raw, x2)[0]
 def shards(adjusted_weight, base_weight, test_matrix):
     delta = adjusted_weight.astype(jnp.float32) - base_weight.astype(jnp.float32)
-    scale_out = jnp.sqrt(jnp.float32(M))
-    own = rs_col(mm(delta, test_matrix))
-    x1 = chol_inverse(gram_blocks(own, 5).reshape(10, B, B))
-    sketch = ag_col(own)
-    raw = rs_row(jnp.einsum("mn,mk->nk", delta, sketch, precision=HI, preferred_element_type=jnp.float32))
-    own_co = apply_inverse(raw, x1)
-    x2 = chol_inverse(gram_blocks(own_co, 6).reshape(10, B, B))
-    cosketch = ag_row(own_co)
-    own = apply_inverse(rs_col(mm(delta, cosketch)), x2)
-    x3 = chol_inverse(gram_blocks(own, 5).reshape(10, B, B))
-    return scale_out * apply_inverse(own, x3)
+    own = col_sum(mm(delta, test_matrix))
+    sketch, g1 = gather_gram(own)
+    raw, x1 = row_sum_chol(jnp.einsum("mn,mk->nk", delta, sketch, precision=HI, preferred_element_type=jnp.float32), g1)
+    cosketch, g2 = norm_gather(raw, x1)
+    raw, x2 = col_sum_chol(mm(delta, cosketch), g2)
+    return last(raw, x2)
 
 
 def solution(mesh):

time: 449 us -> 377 us (0.84)
  Pallas kernels: 317 us -> 255 us
  matrix products: 93.6 us -> 84.9 us
    pallas_call x11 -> x6, Pallas kernels: 317 us -> 255 us  [call(): pl.pallas_call(kernel, out_shape=[jax.ShapeDtypeStruct(s, jnp.float32) fo...]
    dot_general x3 -> x0, matrix products: 8.97 us -> none  [apply_inverse(): lax.dot_general(rows, x, (((1,), (1,)), ((), ())), precision=HI, preferre...]
where the time goes in v2:
time: 377 us; the launch traced here: 370 us
  Pallas kernels  255 us (68%)
  matrix products  84.9 us (23%)
  local copies, waits for them, and re-layouts  16.2 us (4%)
  other arithmetic  13.7 us (4%)
    pallas_call x6, Pallas kernels, call(): pl.pallas_call(kernel, out_shape=[jax.ShapeDtypeStruct(s, jnp.float32) fo...  255 us
    dot_general x2, matrix products, mm(): return jnp.dot(a, b, precision=HI, preferred_element_type=jnp.float32)  56.3 us
    dot_general x1, matrix products, shards(): jnp.einsum('mn,mk->nk', delta, sketch, precision=HI, preferred_element_ty...  28.6 us
    dot_general x1, local copies, waits for them, and re-layouts, shards(): jnp.einsum('mn,mk->nk', delta, sketch, precision=HI, preferred_element_ty...  14.6 us
    dot_general x1, other arithmetic, shards(): jnp.einsum('mn,mk->nk', delta, sketch, precision=HI, preferred_element_ty...  13.7 us

profile of v2, /device:TPU:1, one launch (start us, length us, event | category | flops | bytes accessed | tf_op | source)
XLA Modules:
  0.0 370.4 jit_solution(14984247947858527246)
XLA Ops:
  0.0 0.0 copy-start
  0.0 13.7 %fusion.1 = (f32[1664,2048]{0,1:T(8,128)}, f32[2048,1664]{1,0:T(8,128)}) fusion(bf16[2048,1664]{1,0:T(8,128)(2,1)} %param.4, bf16[2048,1664]{1,0:T(8,128)(2,1)} %param.3), kind=kLoop, calls=%fused_computation.2 | loop fusion | flops 10223616 | bytes 40894464 | tf_op jit(solution)/shard_map/mn,mk->nk/dot_general | solution.py:758
  13.7 14.6 %copy.8 = f32[1664,2048]{1,0:T(8,128)} copy(f32[1664,2048]{0,1:T(8,128)} %get-tuple-element.21) | data formatting | bytes 27262976 | tf_op jit(solution)/shard_map/mn,mk->nk/dot_general | solution.py:758
  28.3 0.0 copy-done
  28.3 27.5 %fusion = f32[2048,512]{1,0:T(8,128)} fusion(f32[1664,512]{1,0:T(8,128)S(1)} %copy-done, bf16[2048,1664]{1,0:T(8,128)(2,1)} %param.4, bf16[2048,1664]{1,0:T(8,128)(2,1)} %param.3), kind=kOutput, calls=%fused_computation.1 | convolution fusion | flops 20948189184 | bytes 21233664 | tf_op jit(solution)/shard_map/dot_general | solution.py:309
  55.8 36.9 %col_sum.1.p = f32[64,512]{1,0:T(8,128)} custom-call(f32[4,2,4,64,512]{4,3,2,1,0:T(8,128)} %bitcast.24), custom_call_target="tpu_custom_call" | custom-call | tf_op jit(solution)/shard_map/col_sum/pallas_call | solution.py:670
  92.7 47.4 %gather_gram.1 = (f32[4,2,4,64,512]{4,3,2,1,0:T(8,128)}, f32[2,5,128,128]{3,2,1,0:T(8,128)}) custom-call(f32[64,512]{1,0:T(8,128)} %col_sum.1.p), custom_call_target="tpu_custom_call" | custom-call | tf_op jit(solution)/shard_map/gather_gram/pallas_call | solution.py:670
  140.1 28.6 %fusion.2.p = f32[2,2,416,512]{3,2,1,0:T(8,128)} fusion(f32[2,2,416,2048]{3,2,1,0:T(8,128)} %bitcast.23, f32[2048,512,1,1]{1,0,3,2:T(8,128)} %bitcast.27), kind=kOutput, calls=%fused_computation.3 | convolution fusion | flops 20937965568 | bytes 21233664 | tf_op jit(solution)/shard_map/mn,mk->nk/dot_general | solution.py:758
  168.7 32.4 %row_sum_chol.1 = (f32[416,512]{1,0:T(8,128)}, f32[512,512]{1,0:T(8,128)}) custom-call(f32[2,2,416,512]{3,2,1,0:T(8,128)} %fusion.2.p, f32[10,128,128]{2,1,0:T(8,128)} %bitcast.26), custom_call_target="tpu_custom_call" | custom-call | tf_op jit(solution)/shard_map/row_sum_chol/pallas_call | solution.py:670
  201.1 46.3 %norm_gather.1 = (f32[2,2,416,512]{3,2,1,0:T(8,128)}, f32[2,5,128,128]{3,2,1,0:T(8,128)}) custom-call(f32[416,512]{1,0:T(8,128)} %get-tuple-element.15.p, f32[512,512]{1,0:T(8,128)} %get-tuple-element.16.x), custom_call_target="tpu_custom_call" | custom-call | tf_op jit(solution)/shard_map/norm_gather/pallas_call | solution.py:670
  247.4 0.0 copy-start.1
  247.4 28.8 %fusion.3.p = f32[4,2,4,64,512]{4,3,2,1,0:T(8,128)} fusion(f32[4,2,4,64,1664]{4,3,2,1,0:T(8,128)} %bitcast.22, f32[1664,512,1,1,1]{1,0,4,3,2:T(8,128)} %bitcast.28), kind=kOutput, calls=%fused_computation.4 | convolution fusion | flops 20937965568 | bytes 21233664 | tf_op jit(solution)/shard_map/dot_general | solution.py:309
  276.3 37.0 %col_sum_chol.1 = (f32[64,512]{1,0:T(8,128)}, f32[512,512]{1,0:T(8,128)}) custom-call(f32[4,2,4,64,512]{4,3,2,1,0:T(8,128)} %fusion.3.p, f32[10,128,128]{2,1,0:T(8,128)} %bitcast.25), custom_call_target="tpu_custom_call" | custom-call | tf_op jit(solution)/shard_map/col_sum_chol/pallas_call | solution.py:670
  313.3 55.3 %last.1 = f32[64,512]{1,0:T(8,128)} custom-call(f32[64,512]{1,0:T(8,128)} %get-tuple-element.19.p, f32[512,512]{1,0:T(8,128)} %get-tuple-element.20.x2), custom_call_target="tpu_custom_call" | custom-call | tf_op jit(solution)/shard_map/last/pallas_call | solution.py:670
  368.6 1.6 copy.12
  370.2 0.0 copy-done.1
Async XLA Ops:
  0.0 28.3 %copy-start = (f32[1664,512]{1,0:T(8,128)S(1)}, f32[1664,512]{1,0:T(8,128)}, u32[]{:S(2)}) copy-start(f32[1664,512]{1,0:T(8,128)} %param.5) | copy-start | bytes 10223620
  247.4 122.8 %copy-start.1 = (f32[1664,512]{1,0:T(8,128)S(1)}, f32[1664,512]{1,0:T(8,128)}, u32[]{:S(2)}) copy-start(f32[1664,512]{1,0:T(8,128)} %param.5) | copy-start | bytes 10223620
